TPU v7x, 32 devices: a whole 2x2x4 slice. The times are simulated.
32 devices in a mesh: pts: 16 (over z, y, x), blk: 2 (over core).
Axes of the slice: x: 2, y: 2, z: 4, core: 2. Of those that a mesh axis runs over, the one named last changes fastest.
Arguments:
- deviations: bfloat16 [196608, 256], P(('pts', 'blk')), may hold values from -6 to 6
- basis: bfloat16 [196608, 64], P(('pts', 'blk')), may hold values from -0.013671875 to 0.013671875
- sensitivity: bfloat16 [64, 512, 512], P('pts', 'blk'), may hold values from -0.75 to 0.75
- blade_ids: int32 [24], replicated, may hold values from 0 to 255, as said below
Outputs:
- gram: float32 [256, 256], P('pts', 'blk')
- change: float32 [24, 512, 512], P(None, 'blk', 'pts')
Inputs may be any that keep to these rules, and one draw needn't show every extreme that they name: `blade_ids`: distinct blade numbers; blade 0 and blade 256 - 1 are always among them.
All inputs are finite; a program needn't handle non-finite values.
Results may differ from a plain program's by a relative error of at most 0.0003.
Values may be sent and summed in bfloat16 or wider, within the bound.
A program may use at most 64 MiB of HBM per device.

v0:
```python
import jax
import jax.numpy as jnp
from jax import lax
from jax.sharding import PartitionSpec as P


def on_device(deviations, basis, sensitivity, blade_ids):
    count_pts = lax.axis_size("pts")
    count_blk = lax.axis_size("blk")
    total = deviations.shape[0] * count_pts * count_blk
    blades = deviations.shape[1]
    dims = (((0,), (0,)), ((), ()))
    term = lax.dot_general(deviations, deviations, dims, preferred_element_type=jnp.float32) / total
    row_part = lax.psum_scatter(term, "pts", scatter_dimension=0, tiled=True)
    gram = lax.psum_scatter(row_part, "blk", scatter_dimension=1, tiled=True)
    coeff_part = lax.dot_general(basis, deviations, dims, preferred_element_type=jnp.float32)
    energy_part = jnp.sum(jnp.square(deviations.astype(jnp.float32)), axis=0) / total
    selector = (jnp.arange(blades, dtype=jnp.int32)[:, None] == blade_ids[None, :]).astype(
        jnp.float32
    )
    coeffs, energy = lax.psum((coeff_part, energy_part), ("pts", "blk"))
    picked = jnp.dot(coeffs, selector, precision=lax.Precision.HIGHEST)
    picked_energy = jnp.dot(energy, selector, precision=lax.Precision.HIGHEST)
    weights = picked / jnp.sqrt(picked_energy + 1e-05)
    tiles = lax.all_to_all(sensitivity, "pts", split_axis=2, concat_axis=0, tiled=True)
    change = jnp.einsum(
        "kb,kij->bij", weights, tiles.astype(jnp.float32), precision=lax.Precision.HIGHEST
    )
    return (gram, change)


def solution(mesh):
    in_specs = (P(("pts", "blk"), None), P(("pts", "blk"), None), P("pts", "blk", None), P())
    out_specs = (P("pts", "blk"), P(None, "blk", "pts"))
    return jax.shard_map(
        on_device, mesh=mesh, in_specs=in_specs, out_specs=out_specs, check_vma=False
    )
```

profile of v0, /device:TPU:0, one launch (start us, length us, event | category | flops | bytes accessed | tf_op | source)
XLA Modules:
  0.0 162.8 jit_solution(8106260641000314574)
XLA Ops:
  8.0 0.0 copy-start
  8.0 2.5 %copy.11 = bf16[4,256,512]{1,0,2:T(4,128)(2,1)} copy(bf16[4,256,512]{2,1,0:T(8,128)(2,1)} %param.6) | data formatting | bytes 2097152 | tf_op args[2]
  10.5 8.3 %all-to-all-start = ((bf16[4,256,512]{1,0,2:T(4,128)(2,1)}), bf16[4,256,512]{1,0,2:T(4,128)(2,1)S(1)}, u32[]{:S(2)}, u32[]{:S(2)}) async-start(bf16[4,256,512]{1,0,2:T(4,128)(2,1)} %copy.11), calls=%async_computation.2 | async-start | bytes 2097152 | tf_op jit(solution)/shard_map/all_to_all | solution.py:25
  18.8 0.0 all-reduce.2.cloned.1.call-start
  18.9 0.0 copy-done
  18.9 3.1 %fusion.5 = f32[64,256]{1,0:T(8,128)} fusion(bf16[6144,64]{0,1:T(8,128)(2,1)S(1)} %copy-done, bf16[6144,256]{1,0:T(8,128)(2,1)} %param.4), kind=kOutput, calls=%fused_computation.11 | convolution fusion | flops 201326592 | bytes 3997696 | tf_op jit(solution)/shard_map/dot_general | solution.py:16
  22.0 0.0 all-reduce.2.cloned.1.call-update
  22.0 0.0 reduce-scatter.3.cloned.1.call-start
  22.1 4.6 %convolution_multiply_fusion = f32[256,256]{1,0:T(8,128)} fusion(bf16[6144,256]{1,0:T(8,128)(2,1)} %param.4), kind=kOutput, calls=%fused_computation.1 | convolution fusion | flops 805371904 | bytes 3407872 | tf_op jit(solution)/shard_map/dot_general | solution.py:13
  26.6 0.0 copy-start.1
  26.6 0.0 reduce-scatter.3.cloned.1.call-update
  26.7 0.0 reduce-scatter.5.cloned.1.call-start
  26.7 2.7 %multiply_reduce_fusion = f32[256]{0:T(256)S(1)} fusion(bf16[6144,256]{1,0:T(8,128)(2,1)} %param.4), kind=kLoop, calls=%fused_computation | loop fusion | flops 4718336 | bytes 3146752 | tf_op jit(solution)/shard_map/reduce_sum | solution.py:17
  29.5 42.4 %psum.15 = f32[256]{0:T(256)S(1)} all-reduce(f32[256]{0:T(256)S(1)} %broadcast_multiply_fusion), channel_id=1, replica_groups=mesh['pts'=16,'blk'=2] {'pts','blk'}, use_global_device_ids=true, to_apply=%region_4.0 | all-reduce | flops 256 | bytes 2048 | tf_op jit(solution)/shard_map/psum | solution.py:21
  71.8 0.0 copy-done.1
  71.8 0.2 fusion.2
  72.0 74.1 %all-reduce.2.cloned.1.call-done = f32[64,256]{1,0:T(8,128)} async-done(((f32[64,256]{1,0:T(8,128)}), f32[64,256]{1,0:T(8,128)}) %all-reduce.2.cloned.1.call-update) | async-done | bytes 65552 | tf_op jit(solution)/shard_map/psum | solution.py:21
  146.0 1.1 fusion
  147.1 0.0 reduce-scatter.3.cloned.1.call-done
  147.2 0.0 reduce-scatter.5.cloned.1.call-update
  147.2 0.0 all-to-all-done
  147.2 0.1 copy.12
  147.3 0.8 copy.13
  148.2 0.3 all_to_all.16
  148.4 0.5 fusion.6
  149.0 1.1 copy.14
  150.1 5.3 %reduce-scatter.5.cloned.1.call-done = f32[16,128]{1,0:T(8,128)} async-done(((f32[16,256]{1,0:T(8,128)}), f32[16,128]{1,0:T(8,128)}) %reduce-scatter.5.cloned.1.call-update) | async-done | bytes 8208 | tf_op jit(solution)/shard_map/reduce_scatter | solution.py:15
  (1 shorter events, 0.0 us)
Async XLA Ops:
  8.0 10.9 %copy-start = (bf16[6144,64]{0,1:T(8,128)(2,1)S(1)}, bf16[6144,64]{0,1:T(8,128)(2,1)}, u32[]{:S(2)}) copy-start(bf16[6144,64]{0,1:T(8,128)(2,1)} %param.5) | copy-start | bytes 2359300
  10.5 136.7 %all-to-all-start = ((bf16[4,256,512]{1,0,2:T(4,128)(2,1)}), bf16[4,256,512]{1,0,2:T(4,128)(2,1)S(1)}, u32[]{:S(2)}, u32[]{:S(2)}) async-start(bf16[4,256,512]{1,0,2:T(4,128)(2,1)} %copy.11), calls=%async_computation.2 | async-start | bytes 2097152 | tf_op jit(solution)/shard_map/all_to_all | solution.py:25
  18.8 127.2 %all-reduce.2.cloned.1.call-start = ((), (), s32[]{:S(2)}) async-start(), calls=%async_computation.5 | async-start | bytes 131072 | tf_op jit(solution)/shard_map/psum | solution.py:21
  22.0 125.1 %reduce-scatter.3.cloned.1.call-start = ((), (), s32[]{:S(2)}) async-start(), calls=%async_computation.3 | async-start | bytes 278528 | tf_op jit(solution)/shard_map/reduce_scatter | solution.py:14
  26.6 45.2 %copy-start.1 = (s32[24]{0:T(128)S(1)}, s32[24]{0:T(128)}, u32[]{:S(2)}) copy-start(s32[24]{0:T(128)} %param.7) | copy-start | bytes 292
  26.7 128.7 %reduce-scatter.5.cloned.1.call-start = ((), (), s32[]{:S(2)}) async-start(), calls=%async_computation.4 | async-start | bytes 24576 | tf_op jit(solution)/shard_map/reduce_scatter | solution.py:15
Sparse Core Ops, SparseCore 0:
  26.1 119.8 all-reduce.1
Sparse Core Ops, SparseCore 1:
  26.7 77.8 reduce-scatter.2
  147.3 8.1 reduce-scatter.4
where the time goes:
time: 163 us
  waiting for transfers between devices  79.4 us (49%)
  blocking collectives  42.4 us (26%)
  between operations  15.6 us (10%)
  matrix products  9.46 us (6%)
  starting transfers between devices  8.44 us (5%)
  local copies, waits for them, and re-layouts  4.84 us (3%)
  other arithmetic  2.74 us (2%)
    psum x1, waiting for transfers between devices, on_device(): coeffs, energy = lax.psum((coeff_part, energy_part), ('pts', 'blk'))  74.1 us
    psum x1, blocking collectives, on_device(): coeffs, energy = lax.psum((coeff_part, energy_part), ('pts', 'blk'))  42.4 us
    all_to_all x1, starting transfers between devices, on_device(): lax.all_to_all(sensitivity, 'pts', split_axis=2, concat_axis=0, tiled=True)  8.31 us
    reduce_scatter x1, waiting for transfers between devices, on_device(): gram = lax.psum_scatter(row_part, 'blk', scatter_dimension=1, tiled=True)  5.28 us
    dot_general x1, matrix products, on_device(): lax.dot_general(deviations, deviations, dims, preferred_element_type=jnp....  4.56 us
    unnamed x6, local copies, waits for them, and re-layouts  3.6 us
  transfers between devices with their start and end apart: 4, of which 2 were waited for; matrix products, arithmetic and copies ran while one was open for 9% of the time, Pallas kernels for 0%

commit v1 on v0

v1 whole, which is shorter than its diff:
```python
import functools

import jax
import jax.numpy as jnp
from jax import lax
from jax.experimental import pallas as pl
from jax.experimental.pallas import tpu as pltpu
from jax.sharding import PartitionSpec as P

MESH = pl.DeviceIdType.MESH
F32 = jnp.float32
BF16 = jnp.bfloat16
GROUP = 16
EPS = 1e-05


def split_of(count):
    inner = 1
    while inner * inner < count:
        inner *= 2
    return count // inner, inner


def kernel(
    dims, ids_ref, dev_hbm, basis_hbm, sens_hbm, gram_ref, change_ref,
    dev_v, basis_v, sens_v, turned, blocks, gram_acc, coef_acc, w_hi, w_lo,
    s1, r1, s2, r2, s3, r3,
    dev_sem, basis_sem, sens_sem, own_sem, a_send, a_recv, c_send, c_recv, x_send, x_recv, z_send, z_recv,
):
    outer, inner, chunks, total = dims
    count = outer * inner
    half = outer // 2
    me = lax.axis_index("pts")
    core = lax.axis_index("blk")
    o, i = me // inner, me % inner
    side = o // half
    reals = ids_ref.shape[1]
    points, blades = dev_hbm.shape
    shapes = basis_hbm.shape[0]
    own, rows, order = sens_hbm.shape
    cols = order // count
    part = points // chunks
    gram_rows, gram_cols = gram_ref.shape
    span = order // 2

    far = pl.multiple_of((1 - side) * span, 128)
    near = pl.multiple_of(side * span, 128)
    loads = []
    for at, start in enumerate((far, near)):
        loads.append(
            pltpu.make_async_copy(
                sens_hbm.at[:, :, pl.ds(start, span)], sens_v.at[:, :, pl.ds(start, span)], sens_sem.at[at]
            )
        )
        loads[-1].start()
    basis_load = pltpu.make_async_copy(basis_hbm, basis_v, basis_sem)
    basis_load.start()

    def dev_load(c):
        at = pl.ds(pl.multiple_of(c * part, part), part)
        return pltpu.make_async_copy(dev_hbm.at[at], dev_v.at[at], dev_sem.at[c])

    for c in range(chunks):
        dev_load(c).start()

    barrier = pltpu.get_barrier_semaphore()
    for d in range(1, count):
        pl.semaphore_signal(barrier, inc=1, device_id=((me + d) % count, core), device_id_type=MESH)
    pl.semaphore_signal(barrier, inc=1, device_id=(me, 1 - core), device_id_type=MESH)

    def turn(start):
        for k in range(own):
            turned[k, pl.ds(start, span), :] = sens_v[k, :, pl.ds(start, span)].T

    def block_to(peer):
        at = pl.ds(pl.multiple_of(peer * cols, cols), cols)
        return pltpu.make_async_remote_copy(
            src_ref=turned.at[:, at, :], dst_ref=blocks.at[me], send_sem=a_send.at[peer], recv_sem=a_recv.at[me],
            device_id=(peer, core), device_id_type=MESH,
        )

    def block_from(peer):
        return pltpu.make_async_remote_copy(
            src_ref=turned.at[:, pl.ds(0, cols), :], dst_ref=blocks.at[peer], send_sem=a_send.at[peer],
            recv_sem=a_recv.at[peer], device_id=(peer, core), device_id_type=MESH,
        )

    far_planes = [(1 - side) * half + (o + e) % half for e in range(half)]
    near_planes = [side * half + (o + e) % half for e in range(half)]

    loads[0].wait()
    turn(far)
    pl.semaphore_wait(barrier, count)
    sent = []
    for plane in far_planes:
        for e in range(inner):
            sent.append(block_to(plane * inner + (i + e) % inner))
            sent[-1].start()
    loads[1].wait()
    turn(near)
    for at, plane in reversed(list(enumerate(near_planes))):
        for e in range(inner):
            if at == 0 and e == 0:
                continue
            sent.append(block_to(plane * inner + (i + e) % inner))
            sent[-1].start()
    mine = pltpu.make_async_copy(
        turned.at[:, pl.ds(pl.multiple_of(me * cols, cols), cols), :], blocks.at[me], own_sem
    )
    mine.start()

    gram_acc[...] = jnp.zeros_like(gram_acc)
    coef_acc[...] = jnp.zeros_like(coef_acc)
    basis_load.wait()

    def accumulate(c, carry):
        dev_load(c).wait()
        start = pl.multiple_of(c * part, part)
        block = dev_v[pl.ds(start, part), :]
        gram_acc[...] += jnp.dot(block.T, block, preferred_element_type=F32)
        coef_acc[0:shapes, :] += jnp.dot(basis_v[:, pl.ds(start, part)], block, preferred_element_type=F32)
        return carry

    lax.fori_loop(0, chunks, accumulate, 0)

    wide = coef_acc.shape[0]
    ids = jnp.broadcast_to(ids_ref[...].astype(F32), (reals, reals))
    square = lax.broadcasted_iota(jnp.int32, (reals, reals), 0) == lax.broadcasted_iota(jnp.int32, (reals, reals), 1)
    ids_col = jnp.sum(jnp.where(square, ids, 0.0), axis=1, keepdims=True)
    lane = lax.broadcasted_iota(jnp.int32, (reals, blades), 1).astype(F32)
    chosen = jnp.where(ids_col == lane, 1.0, 0.0).astype(F32)
    gram = gram_acc[...]
    diagonal = lax.broadcasted_iota(jnp.int32, gram.shape, 0) == lax.broadcasted_iota(jnp.int32, gram.shape, 1)
    squares = jnp.sum(jnp.where(diagonal, gram, 0.0), axis=0, keepdims=True)
    energy = jnp.sum(chosen * squares, axis=1, keepdims=True)
    picked = lax.dot_general(
        chosen, coef_acc[...], (((1,), (1,)), ((), ())), preferred_element_type=F32, precision=lax.Precision.HIGHEST
    )
    place = lax.broadcasted_iota(jnp.int32, (reals, wide), 1)
    picked = jnp.where(place < shapes, picked, energy)

    for h in range(2):
        s1[h, 0:blades, :] = gram[:, h * gram_cols:(h + 1) * gram_cols]
        s1[h, blades:blades + reals, :] = picked
    over = pltpu.make_async_remote_copy(
        src_ref=s1.at[1 - core], dst_ref=r1, send_sem=c_send, recv_sem=c_recv,
        device_id=(me, 1 - core), device_id_type=MESH,
    )
    over.start()
    over.wait_recv()

    body = outer * gram_rows
    tail = s1[core, blades:blades + reals, :] + r1[blades:blades + reals, :]
    for j in range(inner):
        for q in range(outer):
            at = (q * inner + j) * gram_rows
            s2[j, q * gram_rows:(q + 1) * gram_rows, :] = (
                s1[core, at:at + gram_rows, :] + r1[at:at + gram_rows, :]
            )
        s2[j, body:body + reals, :] = tail
    plane_sent = []
    for e in range(1, inner):
        j = (i + e) % inner
        plane_sent.append(
            pltpu.make_async_remote_copy(
                src_ref=s2.at[j], dst_ref=r2.at[i], send_sem=x_send.at[j], recv_sem=x_recv.at[i],
                device_id=(o * inner + j, core), device_id_type=MESH,
            )
        )
        plane_sent[-1].start()
    value = s2[i]
    for e in range(1, inner):
        j = (i + e) % inner
        pltpu.make_async_remote_copy(
            src_ref=s2.at[j], dst_ref=r2.at[j], send_sem=x_send.at[j], recv_sem=x_recv.at[j],
            device_id=(o * inner + j, core), device_id_type=MESH,
        ).wait_recv()
        value = value + r2[j]

    for q in range(outer):
        s3[q, 0:gram_rows, :] = value[q * gram_rows:(q + 1) * gram_rows, :]
        s3[q, gram_rows:gram_rows + reals, :] = value[body:body + reals, :]
    out_sent = []
    for e in range(1, outer):
        q = (o + e) % outer
        out_sent.append(
            pltpu.make_async_remote_copy(
                src_ref=s3.at[q], dst_ref=r3.at[o], send_sem=z_send.at[q], recv_sem=z_recv.at[o],
                device_id=(q * inner + i, core), device_id_type=MESH,
            )
        )
        out_sent[-1].start()
    value = s3[o]
    for e in range(1, outer):
        q = (o + e) % outer
        pltpu.make_async_remote_copy(
            src_ref=s3.at[q], dst_ref=r3.at[q], send_sem=z_send.at[q], recv_sem=z_recv.at[q],
            device_id=(q * inner + i, core), device_id_type=MESH,
        ).wait_recv()
        value = value + r3[q]
    gram_ref[...] = value[0:gram_rows, :] / total

    packed = value[gram_rows:gram_rows + reals, :]
    moved = pltpu.roll(packed, wide - shapes, 1)
    weights = jnp.where(place < shapes, packed / jnp.sqrt(jnp.where(place < shapes, moved, 0.0) / total + EPS), 0.0)
    tall = jnp.broadcast_to(weights[:, None, :], (reals, GROUP, wide)).reshape(reals * GROUP, wide)
    hi = tall.astype(BF16)
    lo = (tall - hi.astype(F32)).astype(BF16)
    long = shapes * GROUP
    spread = (
        lax.broadcasted_iota(jnp.int32, (wide, long), 1) // GROUP == lax.broadcasted_iota(jnp.int32, (wide, long), 0)
    ).astype(F32).astype(BF16)
    keep = (
        lax.broadcasted_iota(jnp.int32, (reals * GROUP, long), 0) % GROUP
        == lax.broadcasted_iota(jnp.int32, (reals * GROUP, long), 1) % GROUP
    )
    w_hi[...] = jnp.where(keep, jnp.dot(hi, spread, preferred_element_type=F32), 0.0).astype(BF16)
    w_lo[...] = jnp.where(keep, jnp.dot(lo, spread, preferred_element_type=F32), 0.0).astype(BF16)

    mine.wait()
    step = inner * own * GROUP
    for at, plane in enumerate(near_planes + far_planes):
        for e in range(inner):
            if at == 0 and e == 0:
                continue
            block_from(plane * inner + (i + e) % inner).wait_recv()
        lanes = pl.ds(pl.multiple_of(plane * step, step), step)
        left_hi, left_lo = w_hi[:, lanes], w_lo[:, lanes]
        for g in range(cols // GROUP):
            here = slice(g * GROUP, (g + 1) * GROUP)
            right = blocks[pl.ds(plane * inner, inner), :, here, :].reshape(step, rows)
            term = jnp.dot(left_hi, right, preferred_element_type=F32) + jnp.dot(
                left_lo, right, preferred_element_type=F32
            )
            term = term.reshape(reals, GROUP, rows)
            if at == 0:
                change_ref[:, here, :] = term
            else:
                change_ref[:, here, :] += term

    over.wait_send()
    for copy in sent + plane_sent + out_sent:
        copy.wait_send()


def in_kernel(deviations, basis, sensitivity, blade_ids):
    count = lax.axis_size("pts")
    cores = lax.axis_size("blk")
    points, blades = deviations.shape
    shapes = basis.shape[1]
    own, rows, order = sensitivity.shape
    reals = blade_ids.shape[0]
    outer, inner = split_of(count)
    cols = order // count
    gram_rows, gram_cols = blades // count, blades // cores
    chunks = 12
    wide = 2 * shapes
    total = float(points * count * cores)
    hbm = pl.BlockSpec(memory_space=pltpu.HBM)
    vmem = pl.BlockSpec(memory_space=pltpu.VMEM)
    sem = pltpu.SemaphoreType.DMA
    body = outer * gram_rows
    flops = 2 * points * blades * (blades + shapes) + 4 * reals * shapes * GROUP * rows * cols
    gram, change = pl.pallas_call(
        functools.partial(kernel, (outer, inner, chunks, total)),
        out_shape=(
            jax.ShapeDtypeStruct((gram_rows, gram_cols), F32),
            jax.ShapeDtypeStruct((reals, cols, rows), F32),
        ),
        in_specs=[vmem, hbm, hbm, hbm],
        out_specs=(vmem, vmem),
        scratch_shapes=[
            pltpu.VMEM((points, blades), BF16),
            pltpu.VMEM((shapes, points), BF16),
            pltpu.VMEM((own, rows, order), BF16),
            pltpu.VMEM((own, order, rows), BF16),
            pltpu.VMEM((count, own, cols, rows), BF16),
            pltpu.VMEM((blades, blades), F32),
            pltpu.VMEM((wide, blades), F32),
            pltpu.VMEM((reals * GROUP, shapes * GROUP), BF16),
            pltpu.VMEM((reals * GROUP, shapes * GROUP), BF16),
            pltpu.VMEM((2, blades + reals, gram_cols), F32),
            pltpu.VMEM((blades + reals, gram_cols), F32),
            pltpu.VMEM((inner, body + reals, gram_cols), F32),
            pltpu.VMEM((inner, body + reals, gram_cols), F32),
            pltpu.VMEM((outer, gram_rows + reals, gram_cols), F32),
            pltpu.VMEM((outer, gram_rows + reals, gram_cols), F32),
            sem((chunks,)), sem, sem((2,)), sem,
            sem((count,)), sem((count,)), sem, sem,
            sem((inner,)), sem((inner,)), sem((outer,)), sem((outer,)),
        ],
        compiler_params=pltpu.CompilerParams(
            collective_id=0, has_side_effects=True, vmem_limit_bytes=60 * 1024 * 1024
        ),
        cost_estimate=pl.CostEstimate(
            flops=flops, transcendentals=0, bytes_accessed=2 * points * (blades + shapes) + 8 * own * rows * order
        ),
    )(blade_ids[None, :], deviations, basis.T, sensitivity)
    return gram, jnp.transpose(change, (0, 2, 1))


def with_collectives(deviations, basis, sensitivity, blade_ids):
    total = deviations.shape[0] * lax.axis_size("pts") * lax.axis_size("blk")
    blades = deviations.shape[1]
    dims = (((0,), (0,)), ((), ()))
    term = lax.dot_general(deviations, deviations, dims, preferred_element_type=F32) / total
    row_part = lax.psum_scatter(term, "pts", scatter_dimension=0, tiled=True)
    gram = lax.psum_scatter(row_part, "blk", scatter_dimension=1, tiled=True)
    coeff_part = lax.dot_general(basis, deviations, dims, preferred_element_type=F32)
    energy_part = jnp.sum(jnp.square(deviations.astype(F32)), axis=0) / total
    selector = (jnp.arange(blades, dtype=jnp.int32)[:, None] == blade_ids[None, :]).astype(F32)
    coeffs, energy = lax.psum((coeff_part, energy_part), ("pts", "blk"))
    picked = jnp.dot(coeffs, selector, precision=lax.Precision.HIGHEST)
    picked_energy = jnp.dot(energy, selector, precision=lax.Precision.HIGHEST)
    weights = picked / jnp.sqrt(picked_energy + EPS)
    tiles = lax.all_to_all(sensitivity, "pts", split_axis=2, concat_axis=0, tiled=True)
    change = jnp.einsum("kb,kij->bij", weights, tiles.astype(F32), precision=lax.Precision.HIGHEST)
    return gram, change


def on_device(deviations, basis, sensitivity, blade_ids):
    count, cores = lax.axis_size("pts"), lax.axis_size("blk")
    points, blades = deviations.shape
    own, rows, order = sensitivity.shape
    outer, inner = split_of(count)
    fits = (
        cores == 2
        and outer * inner == count
        and outer % 2 == 0
        and (order // count) % GROUP == 0
        and (blades // count) % 8 == 0
        and (blades // cores) == 2 * basis.shape[1]
        and (blades // cores) % 128 == 0
        and rows % 128 == 0
        and order % 256 == 0
        and (inner * own * GROUP) % 128 == 0
        and points % (12 * 128) == 0
        and blade_ids.shape[0] % 8 == 0
    )
    run = in_kernel if fits else with_collectives
    return run(deviations, basis, sensitivity, blade_ids)


def solution(mesh):
    in_specs = (P(("pts", "blk"), None), P(("pts", "blk"), None), P("pts", "blk", None), P())
    out_specs = (P("pts", "blk"), P(None, "blk", "pts"))
    return jax.shard_map(
        on_device, mesh=mesh, in_specs=in_specs, out_specs=out_specs, check_vma=False
    )
```

time: 163 us -> 40.3 us (0.25)
  waiting for transfers between devices: 79.4 us -> 0 us
  blocking collectives: 42.4 us -> 0 us
  Pallas kernels: 0 us -> 36.1 us
  between operations: 15.6 us -> 0.64 us
  matrix products: 9.46 us -> 0 us
  starting transfers between devices: 8.44 us -> 0 us
  other arithmetic: 2.74 us -> 0 us
    psum x1 -> x0, waiting for transfers between devices: 74.1 us -> none  [on_device(): coeffs, energy = lax.psum((coeff_part, energy_part), ('pts', 'blk'))]
    psum x1 -> x0, blocking collectives: 42.4 us -> none  [on_device(): coeffs, energy = lax.psum((coeff_part, energy_part), ('pts', 'blk'))]
    pallas_call x0 -> x1, Pallas kernels: none -> 36.1 us  [in_kernel(): pl.pallas_call(functools.partial(kernel, (outer, inner, chunks, total)),...]
    dot_general x5 -> x0, matrix products: 9.46 us -> none  [the longest x1 4.56 us: on_device(): lax.dot_general(deviations, deviations, dims, preferred_element_type=jnp....]
    all_to_all x1 -> x0, starting transfers between devices: 8.31 us -> none  [on_device(): lax.all_to_all(sensitivity, 'pts', split_axis=2, concat_axis=0, tiled=True)]
    reduce_scatter x2 -> x0, waiting for transfers between devices: 5.3 us -> none  [the longest x1 5.28 us: on_device(): gram = lax.psum_scatter(row_part, 'blk', scatter_dimension=1, tiled=True)]
    reduce_sum x1 -> x0, other arithmetic: 2.73 us -> none  [on_device(): jnp.sum(jnp.square(deviations.astype(jnp.float32)), axis=0) / total]
    unnamed x6 -> x2, local copies, waits for them, and re-layouts: 3.6 us -> 3.38 us
  transfers between devices with their start and end apart: 4 -> 0, of which waited for: 2 -> 0; matrix products, arithmetic and copies ran while one was open for 9% -> 0% of each run, Pallas kernels for 0% -> 0%
where the time goes in v1:
time: 40.3 us; the launch traced here: 40.1 us
  Pallas kernels  36.1 us (90%)
  local copies, waits for them, and re-layouts  3.38 us (8%)
  between operations  0.64 us (2%)
    pallas_call x1, Pallas kernels, in_kernel(): pl.pallas_call(functools.partial(kernel, (outer, inner, chunks, total)),...  36.1 us
    unnamed x2, local copies, waits for them, and re-layouts  3.38 us

profile of v1, /device:TPU:0, one launch (start us, length us, event | category | flops | bytes accessed | tf_op | source)
XLA Modules:
  0.0 40.1 jit_solution(11880794995483049801)
XLA Ops:
  0.6 36.1 %shard_map.59 = (f32[16,128]{1,0:T(8,128)}, f32[24,32,256]{2,1,0:T(8,128)}) custom-call(s32[1,24]{1,0:T(1,128)} %bitcast.5, bf16[6144,256]{1,0:T(8,128)(2,1)} %dev_hbm.1, bf16[64,6144]{1,0:T(8,128)(2,1)} %bitcast.4, bf16[4,256,512]{2,1,0:T(8,128)(2,1)} %sens_hbm.1), custom_call_target="tpu_custom_call" | custom-call | flops 1811939328 | bytes 8126464 | tf_op jit(solution)/shard_map/pallas_call | solution.py:264
  36.7 1.3 %copy.8 = f32[16,128]{1,0:T(8,128)} copy(f32[16,128]{1,0:T(8,128)} %get-tuple-element.8) | data formatting | bytes 16384
  38.0 2.1 %copy.9 = f32[24,256,32]{1,2,0:T(8,128)} copy(f32[24,256,32]{1,2,0:T(8,128)} %bitcast.3) | data formatting | bytes 1572864

commit v2 on v1

--- a/solution.py
+++ b/solution.py
@@ -22,10 +22,10 @@
 
 
 def kernel(
-    dims, ids_ref, dev_hbm, basis_hbm, sens_hbm, gram_ref, change_ref,
-    dev_v, basis_v, sens_v, turned, blocks, gram_acc, coef_acc, w_hi, w_lo,
+    dims, ids_hbm, dev_hbm, basis_hbm, sens_hbm, gram_ref, change_ref,
+    ids_ref, dev_v, basis_v, sens_v, turned, blocks, gram_acc, coef_acc, spread_v, keep_v, w_hi, w_lo,
     s1, r1, s2, r2, s3, r3,
-    dev_sem, basis_sem, sens_sem, own_sem, a_send, a_recv, c_send, c_recv, x_send, x_recv, z_send, z_recv,
+    ids_sem, dev_sem, basis_sem, sens_sem, own_sem, a_send, a_recv, c_send, c_recv, x_send, x_recv, z_send, z_recv,
 ):
     outer, inner, chunks, total = dims
     count = outer * inner
@@ -43,6 +43,11 @@
     gram_rows, gram_cols = gram_ref.shape
     span = order // 2
 
+    barrier = pltpu.get_barrier_semaphore()
+    for d in range(1, count):
+        pl.semaphore_signal(barrier, inc=1, device_id=((me + d) % count, core), device_id_type=MESH)
+    pl.semaphore_signal(barrier, inc=1, device_id=(me, 1 - core), device_id_type=MESH)
+
     far = pl.multiple_of((1 - side) * span, 128)
     near = pl.multiple_of(side * span, 128)
     loads = []
@@ -53,6 +58,8 @@
             )
         )
         loads[-1].start()
+    ids_load = pltpu.make_async_copy(ids_hbm, ids_ref, ids_sem)
+    ids_load.start()
     basis_load = pltpu.make_async_copy(basis_hbm, basis_v, basis_sem)
     basis_load.start()
 
@@ -62,11 +69,6 @@
 
     for c in range(chunks):
         dev_load(c).start()
-
-    barrier = pltpu.get_barrier_semaphore()
-    for d in range(1, count):
-        pl.semaphore_signal(barrier, inc=1, device_id=((me + d) % count, core), device_id_type=MESH)
-    pl.semaphore_signal(barrier, inc=1, device_id=(me, 1 - core), device_id_type=MESH)
 
     def turn(start):
         for k in range(own):
@@ -109,6 +111,14 @@
     )
     mine.start()
 
+    spread_v[...] = (
+        lax.broadcasted_iota(jnp.int32, spread_v.shape, 1) // GROUP == lax.broadcasted_iota(jnp.int32, spread_v.shape, 0)
+    ).astype(F32).astype(BF16)
+    keep_v[...] = (
+        lax.broadcasted_iota(jnp.int32, keep_v.shape, 0) % GROUP
+        == lax.broadcasted_iota(jnp.int32, keep_v.shape, 1) % GROUP
+    ).astype(F32).astype(BF16)
+
     gram_acc[...] = jnp.zeros_like(gram_acc)
     coef_acc[...] = jnp.zeros_like(coef_acc)
     basis_load.wait()
@@ -124,6 +134,7 @@
     lax.fori_loop(0, chunks, accumulate, 0)
 
     wide = coef_acc.shape[0]
+    ids_load.wait()
     ids = jnp.broadcast_to(ids_ref[...].astype(F32), (reals, reals))
     square = lax.broadcasted_iota(jnp.int32, (reals, reals), 0) == lax.broadcasted_iota(jnp.int32, (reals, reals), 1)
     ids_col = jnp.sum(jnp.where(square, ids, 0.0), axis=1, keepdims=True)
@@ -206,16 +217,9 @@
     tall = jnp.broadcast_to(weights[:, None, :], (reals, GROUP, wide)).reshape(reals * GROUP, wide)
     hi = tall.astype(BF16)
     lo = (tall - hi.astype(F32)).astype(BF16)
-    long = shapes * GROUP
-    spread = (
-        lax.broadcasted_iota(jnp.int32, (wide, long), 1) // GROUP == lax.broadcasted_iota(jnp.int32, (wide, long), 0)
-    ).astype(F32).astype(BF16)
-    keep = (
-        lax.broadcasted_iota(jnp.int32, (reals * GROUP, long), 0) % GROUP
-        == lax.broadcasted_iota(jnp.int32, (reals * GROUP, long), 1) % GROUP
-    )
-    w_hi[...] = jnp.where(keep, jnp.dot(hi, spread, preferred_element_type=F32), 0.0).astype(BF16)
-    w_lo[...] = jnp.where(keep, jnp.dot(lo, spread, preferred_element_type=F32), 0.0).astype(BF16)
+    spread = spread_v[...]
+    w_hi[...] = jnp.dot(hi, spread, preferred_element_type=F32).astype(BF16) * keep_v[...]
+    w_lo[...] = jnp.dot(lo, spread, preferred_element_type=F32).astype(BF16) * keep_v[...]
 
     mine.wait()
     step = inner * own * GROUP
@@ -241,6 +245,18 @@
     over.wait_send()
     for copy in sent + plane_sent + out_sent:
         copy.wait_send()
+
+
+def hand_over(pieces, gram_ref, change_ref, gram_out, change_out, sems):
+    part = change_ref.shape[0] // pieces
+    copies = [pltpu.make_async_copy(gram_ref, gram_out, sems.at[pieces])]
+    for at in range(pieces):
+        here = pl.ds(at * part, part)
+        copies.append(pltpu.make_async_copy(change_ref.at[here], change_out.at[here], sems.at[at]))
+    for copy in copies:
+        copy.start()
+    for copy in copies:
+        copy.wait()
 
 
 def in_kernel(deviations, basis, sensitivity, blade_ids):
@@ -263,13 +279,11 @@
     flops = 2 * points * blades * (blades + shapes) + 4 * reals * shapes * GROUP * rows * cols
     gram, change = pl.pallas_call(
         functools.partial(kernel, (outer, inner, chunks, total)),
-        out_shape=(
-            jax.ShapeDtypeStruct((gram_rows, gram_cols), F32),
-            jax.ShapeDtypeStruct((reals, cols, rows), F32),
-        ),
-        in_specs=[vmem, hbm, hbm, hbm],
+        out_shape=(pltpu.VMEM((gram_rows, gram_cols), F32), pltpu.VMEM((reals, cols, rows), F32)),
+        in_specs=[hbm, hbm, hbm, hbm],
         out_specs=(vmem, vmem),
         scratch_shapes=[
+            pltpu.VMEM((1, reals), jnp.int32),
             pltpu.VMEM((points, blades), BF16),
             pltpu.VMEM((shapes, points), BF16),
             pltpu.VMEM((own, rows, order), BF16),
@@ -277,6 +291,8 @@
             pltpu.VMEM((count, own, cols, rows), BF16),
             pltpu.VMEM((blades, blades), F32),
             pltpu.VMEM((wide, blades), F32),
+            pltpu.VMEM((wide, shapes * GROUP), BF16),
+            pltpu.VMEM((reals * GROUP, shapes * GROUP), BF16),
             pltpu.VMEM((reals * GROUP, shapes * GROUP), BF16),
             pltpu.VMEM((reals * GROUP, shapes * GROUP), BF16),
             pltpu.VMEM((2, blades + reals, gram_cols), F32),
@@ -285,17 +301,33 @@
             pltpu.VMEM((inner, body + reals, gram_cols), F32),
             pltpu.VMEM((outer, gram_rows + reals, gram_cols), F32),
             pltpu.VMEM((outer, gram_rows + reals, gram_cols), F32),
-            sem((chunks,)), sem, sem((2,)), sem,
+            sem, sem((chunks,)), sem, sem((2,)), sem,
             sem((count,)), sem((count,)), sem, sem,
             sem((inner,)), sem((inner,)), sem((outer,)), sem((outer,)),
         ],
         compiler_params=pltpu.CompilerParams(
-            collective_id=0, has_side_effects=True, vmem_limit_bytes=60 * 1024 * 1024
+            collective_id=0, has_side_effects=True, vmem_limit_bytes=32 * 1024 * 1024
         ),
         cost_estimate=pl.CostEstimate(
             flops=flops, transcendentals=0, bytes_accessed=2 * points * (blades + shapes) + 8 * own * rows * order
         ),
-    )(blade_ids[None, :], deviations, basis.T, sensitivity)
+    )(
+        pltpu.with_memory_space_constraint(blade_ids[None, :], pltpu.HBM),
+        pltpu.with_memory_space_constraint(deviations, pltpu.HBM),
+        pltpu.with_memory_space_constraint(basis.T, pltpu.HBM),
+        pltpu.with_memory_space_constraint(sensitivity, pltpu.HBM),
+    )
+    pieces = 4
+    gram, change = pl.pallas_call(
+        functools.partial(hand_over, pieces),
+        out_shape=(
+            jax.ShapeDtypeStruct((gram_rows, gram_cols), F32),
+            jax.ShapeDtypeStruct((reals, cols, rows), F32),
+        ),
+        in_specs=[vmem, vmem],
+        out_specs=(hbm, hbm),
+        scratch_shapes=[sem((pieces + 1,))],
+    )(gram, change)
     return gram, jnp.transpose(change, (0, 2, 1))
 
 

time: 40.3 us -> 39 us (0.968)
  local copies, waits for them, and re-layouts: 3.38 us -> 1.47 us
  Pallas kernels: 36.1 us -> 36.7 us
    pallas_call x0 -> x1, Pallas kernels: none -> 2.07 us  [in_kernel(): pl.pallas_call(functools.partial(hand_over, pieces), out_shape=(jax.Shape...]
    unnamed x2 -> x4, local copies, waits for them, and re-layouts: 3.38 us -> 1.47 us
    pallas_call x1, Pallas kernels: 36.1 us -> 34.6 us  [in_kernel(): pl.pallas_call(functools.partial(kernel, (outer, inner, chunks, total)),...]
where the time goes in v2:
time: 39 us; the launch traced here: 38.8 us
  Pallas kernels  36.7 us (94%)
  local copies, waits for them, and re-layouts  1.47 us (4%)
  between operations  0.65 us (2%)
    pallas_call x1, Pallas kernels, in_kernel(): pl.pallas_call(functools.partial(kernel, (outer, inner, chunks, total)),...  34.6 us
    pallas_call x1, Pallas kernels, in_kernel(): pl.pallas_call(functools.partial(hand_over, pieces), out_shape=(jax.Shape...  2.07 us
    unnamed x4, local copies, waits for them, and re-layouts  1.47 us

profile of v2, /device:TPU:0, one launch (start us, length us, event | category | flops | bytes accessed | tf_op | source)
XLA Modules:
  0.0 38.8 jit_solution(6896649795684772392)
XLA Ops:
  0.6 34.6 %shard_map.59 = (f32[16,128]{1,0:T(8,128)S(1)}, f32[24,32,256]{2,1,0:T(8,128)S(1)}) custom-call(s32[1,24]{1,0:T(1,128)} %bitcast.5, bf16[6144,256]{1,0:T(8,128)(2,1)} %dev_hbm.1, bf16[64,6144]{1,0:T(8,128)(2,1)} %bitcast.3, bf16[4,256,512]{2,1,0:T(8,128)(2,1)} %sens_hbm.1), custom_call_target="tpu_custom_call" | custom-call | flops 1811939328 | bytes 8126464 | tf_op jit(solution)/shard_map/pallas_call | solution.py:280
  35.2 0.0 copy-start
  35.2 0.9 %copy-done = f32[24,32,256]{2,1,0:T(8,128)} copy-done((f32[24,32,256]{2,1,0:T(8,128)}, f32[24,32,256]{2,1,0:T(8,128)S(1)}, u32[]{:S(2)}) %copy-start) | copy-done | bytes 786456
  36.1 0.0 copy-start.1
  36.1 0.6 %copy-done.1 = f32[16,128]{1,0:T(8,128)} copy-done((f32[16,128]{1,0:T(8,128)}, f32[16,128]{1,0:T(8,128)S(1)}, u32[]{:S(2)}) %copy-start.1) | copy-done | bytes 8216
  36.7 2.1 %shard_map.60 = (f32[16,128]{1,0:T(8,128)}, f32[24,32,256]{2,1,0:T(8,128)}) custom-call(f32[16,128]{1,0:T(8,128)} %copy-done.1, f32[24,32,256]{2,1,0:T(8,128)} %copy-done), custom_call_target="tpu_custom_call" | custom-call | tf_op jit(solution)/shard_map/pallas_call | solution.py:321
Async XLA Ops:
  35.2 0.9 %copy-start = (f32[24,32,256]{2,1,0:T(8,128)}, f32[24,32,256]{2,1,0:T(8,128)S(1)}, u32[]{:S(2)}) copy-start(f32[24,32,256]{2,1,0:T(8,128)S(1)} %get-tuple-element.7.change_ref) | copy-start | bytes 2359300
  36.1 0.6 %copy-start.1 = (f32[16,128]{1,0:T(8,128)}, f32[16,128]{1,0:T(8,128)S(1)}, u32[]{:S(2)}) copy-start(f32[16,128]{1,0:T(8,128)S(1)} %get-tuple-element.6.gram_ref) | copy-start | bytes 24580

commit v3 on v2

--- a/solution.py
+++ b/solution.py
@@ -94,10 +94,10 @@
     turn(far)
     pl.semaphore_wait(barrier, count)
     sent = []
-    for plane in far_planes:
-        for e in range(inner):
-            sent.append(block_to(plane * inner + (i + e) % inner))
-            sent[-1].start()
+    crossing = [block_to(plane * inner + (i + e) % inner) for plane in far_planes for e in range(inner)]
+    held = inner // 2
+    for copy in crossing[:-held]:
+        copy.start()
     loads[1].wait()
     turn(near)
     for at, plane in reversed(list(enumerate(near_planes))):
@@ -201,6 +201,8 @@
             )
         )
         out_sent[-1].start()
+    for copy in crossing[-held:]:
+        copy.start()
     value = s3[o]
     for e in range(1, outer):
         q = (o + e) % outer
@@ -243,7 +245,7 @@
                 change_ref[:, here, :] += term
 
     over.wait_send()
-    for copy in sent + plane_sent + out_sent:
+    for copy in crossing + sent + plane_sent + out_sent:
         copy.wait_send()
 
 
@@ -327,7 +329,11 @@
         in_specs=[vmem, vmem],
         out_specs=(hbm, hbm),
         scratch_shapes=[sem((pieces + 1,))],
-    )(gram, change)
+        compiler_params=pltpu.CompilerParams(vmem_limit_bytes=4 * 1024 * 1024),
+    )(
+        pltpu.with_memory_space_constraint(gram, pltpu.VMEM),
+        pltpu.with_memory_space_constraint(change, pltpu.VMEM),
+    )
     return gram, jnp.transpose(change, (0, 2, 1))
 
 

time: 39 us -> 33.4 us (0.86)
  Pallas kernels: 36.7 us -> 32.6 us
  local copies, waits for them, and re-layouts: 1.47 us -> 0 us
    pallas_call x1, Pallas kernels: 34.6 us -> 31.7 us  [in_kernel(): pl.pallas_call(functools.partial(kernel, (outer, inner, chunks, total)),...]
    unnamed x4 -> x0, local copies, waits for them, and re-layouts: 1.47 us -> none
    pallas_call x1, Pallas kernels: 2.07 us -> 0.92 us  [in_kernel(): pl.pallas_call(functools.partial(hand_over, pieces), out_shape=(jax.Shape...]
where the time goes in v3:
time: 33.4 us; the launch traced here: 33.3 us
  Pallas kernels  32.6 us (98%)
  between operations  0.64 us (2%)
    pallas_call x1, Pallas kernels, in_kernel(): pl.pallas_call(functools.partial(kernel, (outer, inner, chunks, total)),...  31.7 us
    pallas_call x1, Pallas kernels, in_kernel(): pl.pallas_call(functools.partial(hand_over, pieces), out_shape=(jax.Shape...  0.92 us

profile of v3, /device:TPU:0, one launch (start us, length us, event | category | flops | bytes accessed | tf_op | source)
XLA Modules:
  0.0 33.3 jit_solution(6904024936300923425)
XLA Ops:
  0.6 31.7 %shard_map.59 = (f32[16,128]{1,0:T(8,128)S(1)}, f32[24,32,256]{2,1,0:T(8,128)S(1)}) custom-call(s32[1,24]{1,0:T(1,128)} %bitcast.5, bf16[6144,256]{1,0:T(8,128)(2,1)} %dev_hbm.1, bf16[64,6144]{1,0:T(8,128)(2,1)} %bitcast.3, bf16[4,256,512]{2,1,0:T(8,128)(2,1)} %sens_hbm.1), custom_call_target="tpu_custom_call" | custom-call | flops 1811939328 | bytes 8126464 | tf_op jit(solution)/shard_map/pallas_call | solution.py:282
  32.3 0.9 %shard_map.60 = (f32[16,128]{1,0:T(8,128)}, f32[24,32,256]{2,1,0:T(8,128)}) custom-call(f32[16,128]{1,0:T(8,128)S(1)} %get-tuple-element.6.gram_ref, f32[24,32,256]{2,1,0:T(8,128)S(1)} %get-tuple-element.7.change_ref), custom_call_target="tpu_custom_call" | custom-call | tf_op jit(solution)/shard_map/pallas_call | solution.py:323

commit v4 on v3

--- a/solution.py
+++ b/solution.py
@@ -41,22 +41,19 @@
     cols = order // count
     part = points // chunks
     gram_rows, gram_cols = gram_ref.shape
-    span = order // 2
+    span = cols * inner
 
     barrier = pltpu.get_barrier_semaphore()
     for d in range(1, count):
         pl.semaphore_signal(barrier, inc=1, device_id=((me + d) % count, core), device_id_type=MESH)
     pl.semaphore_signal(barrier, inc=1, device_id=(me, 1 - core), device_id_type=MESH)
 
-    far = pl.multiple_of((1 - side) * span, 128)
-    near = pl.multiple_of(side * span, 128)
+    far_planes = [(1 - side) * half + (o + e) % half for e in range(half)]
+    near_planes = [side * half + (o + e) % half for e in range(half)]
     loads = []
-    for at, start in enumerate((far, near)):
-        loads.append(
-            pltpu.make_async_copy(
-                sens_hbm.at[:, :, pl.ds(start, span)], sens_v.at[:, :, pl.ds(start, span)], sens_sem.at[at]
-            )
-        )
+    for at, plane in enumerate(far_planes + near_planes):
+        here = pl.ds(pl.multiple_of(plane * span, span), span)
+        loads.append(pltpu.make_async_copy(sens_hbm.at[:, :, here], sens_v.at[:, :, here], sens_sem.at[at]))
         loads[-1].start()
     ids_load = pltpu.make_async_copy(ids_hbm, ids_ref, ids_sem)
     ids_load.start()
@@ -70,9 +67,10 @@
     for c in range(chunks):
         dev_load(c).start()
 
-    def turn(start):
+    def turn(plane):
+        here = pl.ds(pl.multiple_of(plane * span, span), span)
         for k in range(own):
-            turned[k, pl.ds(start, span), :] = sens_v[k, :, pl.ds(start, span)].T
+            turned[k, here, :] = sens_v[k, :, here].T
 
     def block_to(peer):
         at = pl.ds(pl.multiple_of(peer * cols, cols), cols)
@@ -87,20 +85,19 @@
             recv_sem=a_recv.at[peer], device_id=(peer, core), device_id_type=MESH,
         )
 
-    far_planes = [(1 - side) * half + (o + e) % half for e in range(half)]
-    near_planes = [side * half + (o + e) % half for e in range(half)]
-
-    loads[0].wait()
-    turn(far)
-    pl.semaphore_wait(barrier, count)
+    crossing = [block_to(plane * inner + (i + e) % inner) for plane in far_planes for e in range(inner)]
+    early = len(crossing) - inner
+    for at, plane in enumerate(far_planes):
+        loads[at].wait()
+        turn(plane)
+        if at == 0:
+            pl.semaphore_wait(barrier, count)
+        for copy in crossing[at * inner:min((at + 1) * inner, early)]:
+            copy.start()
     sent = []
-    crossing = [block_to(plane * inner + (i + e) % inner) for plane in far_planes for e in range(inner)]
-    held = inner // 2
-    for copy in crossing[:-held]:
-        copy.start()
-    loads[1].wait()
-    turn(near)
     for at, plane in reversed(list(enumerate(near_planes))):
+        loads[half + at].wait()
+        turn(plane)
         for e in range(inner):
             if at == 0 and e == 0:
                 continue
@@ -201,7 +198,7 @@
             )
         )
         out_sent[-1].start()
-    for copy in crossing[-held:]:
+    for copy in crossing[early:]:
         copy.start()
     value = s3[o]
     for e in range(1, outer):
@@ -303,7 +300,7 @@
             pltpu.VMEM((inner, body + reals, gram_cols), F32),
             pltpu.VMEM((outer, gram_rows + reals, gram_cols), F32),
             pltpu.VMEM((outer, gram_rows + reals, gram_cols), F32),
-            sem, sem((chunks,)), sem, sem((2,)), sem,
+            sem, sem((chunks,)), sem, sem((outer,)), sem,
             sem((count,)), sem((count,)), sem, sem,
             sem((inner,)), sem((inner,)), sem((outer,)), sem((outer,)),
         ],
@@ -370,7 +367,7 @@
         and (blades // cores) == 2 * basis.shape[1]
         and (blades // cores) % 128 == 0
         and rows % 128 == 0
-        and order % 256 == 0
+        and (order // count * inner) % 128 == 0
         and (inner * own * GROUP) % 128 == 0
         and points % (12 * 128) == 0
         and blade_ids.shape[0] % 8 == 0

time: 33.4 us -> 35.2 us (1.054)
  the two profiles are of different devices: /device:TPU:0 before, /device:TPU:11 now
where the time goes in v4:
time: 35.2 us; the launch traced here: 35.1 us
  Pallas kernels  34.4 us (98%)
  between operations  0.64 us (2%)
    pallas_call x1, Pallas kernels, in_kernel(): pl.pallas_call(functools.partial(kernel, (outer, inner, chunks, total)),...  33.5 us
    pallas_call x1, Pallas kernels, in_kernel(): pl.pallas_call(functools.partial(hand_over, pieces), out_shape=(jax.Shape...  0.92 us

profile of v4, /device:TPU:11, one launch (start us, length us, event | category | flops | bytes accessed | tf_op | source)
XLA Modules:
  0.0 35.1 jit_solution(17686469945988745460)
XLA Ops:
  0.6 33.5 %shard_map.59 = (f32[16,128]{1,0:T(8,128)S(1)}, f32[24,32,256]{2,1,0:T(8,128)S(1)}) custom-call(s32[1,24]{1,0:T(1,128)} %bitcast.5, bf16[6144,256]{1,0:T(8,128)(2,1)} %dev_hbm.1, bf16[64,6144]{1,0:T(8,128)(2,1)} %bitcast.3, bf16[4,256,512]{2,1,0:T(8,128)(2,1)} %sens_hbm.1), custom_call_target="tpu_custom_call" | custom-call | flops 1811939328 | bytes 8126464 | tf_op jit(solution)/shard_map/pallas_call | solution.py:279
  34.1 0.9 %shard_map.60 = (f32[16,128]{1,0:T(8,128)}, f32[24,32,256]{2,1,0:T(8,128)}) custom-call(f32[16,128]{1,0:T(8,128)S(1)} %get-tuple-element.6.gram_ref, f32[24,32,256]{2,1,0:T(8,128)S(1)} %get-tuple-element.7.change_ref), custom_call_target="tpu_custom_call" | custom-call | tf_op jit(solution)/shard_map/pallas_call | solution.py:320

commit v5 on v4

--- a/solution.py
+++ b/solution.py
@@ -86,7 +86,7 @@
         )
 
     crossing = [block_to(plane * inner + (i + e) % inner) for plane in far_planes for e in range(inner)]
-    early = len(crossing) - inner
+    early = len(crossing) - (inner - 1)
     for at, plane in enumerate(far_planes):
         loads[at].wait()
         turn(plane)
@@ -102,7 +102,6 @@
             if at == 0 and e == 0:
                 continue
             sent.append(block_to(plane * inner + (i + e) % inner))
-            sent[-1].start()
     mine = pltpu.make_async_copy(
         turned.at[:, pl.ds(pl.multiple_of(me * cols, cols), cols), :], blocks.at[me], own_sem
     )
@@ -176,6 +175,8 @@
             )
         )
         plane_sent[-1].start()
+    for copy in sent:
+        copy.start()
     value = s2[i]
     for e in range(1, inner):
         j = (i + e) % inner

time: 35.2 us -> 35.5 us (level)
  the two profiles are of different devices: /device:TPU:11 before, /device:TPU:0 now
where the time goes in v5:
time: 35.5 us; the launch traced here: 35.4 us
  Pallas kernels  34.7 us (98%)
  between operations  0.64 us (2%)
    pallas_call x1, Pallas kernels, in_kernel(): pl.pallas_call(functools.partial(kernel, (outer, inner, chunks, total)),...  33.8 us
    pallas_call x1, Pallas kernels, in_kernel(): pl.pallas_call(functools.partial(hand_over, pieces), out_shape=(jax.Shape...  0.92 us

profile of v5, /device:TPU:0, one launch (start us, length us, event | category | flops | bytes accessed | tf_op | source)
XLA Modules:
  0.0 35.4 jit_solution(3079541762959449670)
XLA Ops:
  0.6 33.8 %shard_map.59 = (f32[16,128]{1,0:T(8,128)S(1)}, f32[24,32,256]{2,1,0:T(8,128)S(1)}) custom-call(s32[1,24]{1,0:T(1,128)} %bitcast.5, bf16[6144,256]{1,0:T(8,128)(2,1)} %dev_hbm.1, bf16[64,6144]{1,0:T(8,128)(2,1)} %bitcast.3, bf16[4,256,512]{2,1,0:T(8,128)(2,1)} %sens_hbm.1), custom_call_target="tpu_custom_call" | custom-call | flops 1811939328 | bytes 8126464 | tf_op jit(solution)/shard_map/pallas_call | solution.py:280
  34.4 0.9 %shard_map.60 = (f32[16,128]{1,0:T(8,128)}, f32[24,32,256]{2,1,0:T(8,128)}) custom-call(f32[16,128]{1,0:T(8,128)S(1)} %get-tuple-element.6.gram_ref, f32[24,32,256]{2,1,0:T(8,128)S(1)} %get-tuple-element.7.change_ref), custom_call_target="tpu_custom_call" | custom-call | tf_op jit(solution)/shard_map/pallas_call | solution.py:321

commit v6 on v4

--- a/solution.py
+++ b/solution.py
@@ -50,8 +50,12 @@
 
     far_planes = [(1 - side) * half + (o + e) % half for e in range(half)]
     near_planes = [side * half + (o + e) % half for e in range(half)]
+    depth = side * (o - half) + (1 - side) * (half - 1 - o)
+    middle = 1 - (2 * depth) // half
+    first = [middle * n + (1 - middle) * f for n, f in zip(near_planes, far_planes)]
+    second = [middle * f + (1 - middle) * n for n, f in zip(near_planes, far_planes)]
     loads = []
-    for at, plane in enumerate(far_planes + near_planes):
+    for at, plane in enumerate(first + second):
         here = pl.ds(pl.multiple_of(plane * span, span), span)
         loads.append(pltpu.make_async_copy(sens_hbm.at[:, :, here], sens_v.at[:, :, here], sens_sem.at[at]))
         loads[-1].start()
@@ -86,23 +90,28 @@
         )
 
     crossing = [block_to(plane * inner + (i + e) % inner) for plane in far_planes for e in range(inner)]
-    early = len(crossing) - inner
-    for at, plane in enumerate(far_planes):
+    inside = [
+        [block_to(plane * inner + (i + e) % inner) for e in range(inner) if at > 0 or e > 0]
+        for at, plane in enumerate(near_planes)
+    ]
+    many = len(crossing)
+
+    def send(outside_copies, middle_copies):
+        for kind, copies in ((0, outside_copies), (1, middle_copies)):
+            @pl.when(middle == kind)
+            def _():
+                for copy in copies:
+                    copy.start()
+
+    for at, plane in enumerate(first):
         loads[at].wait()
         turn(plane)
         if at == 0:
             pl.semaphore_wait(barrier, count)
-        for copy in crossing[at * inner:min((at + 1) * inner, early)]:
-            copy.start()
-    sent = []
-    for at, plane in reversed(list(enumerate(near_planes))):
+        send(crossing[at * inner:min((at + 1) * inner, many // 2)], inside[at])
+    for at, plane in enumerate(second):
         loads[half + at].wait()
         turn(plane)
-        for e in range(inner):
-            if at == 0 and e == 0:
-                continue
-            sent.append(block_to(plane * inner + (i + e) % inner))
-            sent[-1].start()
     mine = pltpu.make_async_copy(
         turned.at[:, pl.ds(pl.multiple_of(me * cols, cols), cols), :], blocks.at[me], own_sem
     )
@@ -155,6 +164,7 @@
         device_id=(me, 1 - core), device_id_type=MESH,
     )
     over.start()
+    send(crossing[many // 2:3 * many // 4], crossing[:many // 8])
     over.wait_recv()
 
     body = outer * gram_rows
@@ -176,6 +186,7 @@
             )
         )
         plane_sent[-1].start()
+    send(crossing[3 * many // 4:7 * many // 8], crossing[many // 8:many // 4])
     value = s2[i]
     for e in range(1, inner):
         j = (i + e) % inner
@@ -198,8 +209,7 @@
             )
         )
         out_sent[-1].start()
-    for copy in crossing[early:]:
-        copy.start()
+    send(crossing[7 * many // 8:] + sum(inside, []), crossing[many // 4:])
     value = s3[o]
     for e in range(1, outer):
         q = (o + e) % outer
@@ -222,7 +232,8 @@
 
     mine.wait()
     step = inner * own * GROUP
-    for at, plane in enumerate(near_planes + far_planes):
+    last_planes = [side * e + (1 - side) * (outer - 1 - e) for e in range(half)]
+    for at, plane in enumerate(near_planes + last_planes):
         for e in range(inner):
             if at == 0 and e == 0:
                 continue
@@ -242,7 +253,7 @@
                 change_ref[:, here, :] += term
 
     over.wait_send()
-    for copy in crossing + sent + plane_sent + out_sent:
+    for copy in crossing + sum(inside, []) + plane_sent + out_sent:
         copy.wait_send()
 
 

time: 35.2 us -> 34.1 us (0.969)
  the two profiles are of different devices: /device:TPU:11 before, /device:TPU:10 now
where the time goes in v6:
time: 34.1 us; the launch traced here: 33.9 us
  Pallas kernels  33.3 us (98%)
  between operations  0.64 us (2%)
    pallas_call x1, Pallas kernels, in_kernel(): pl.pallas_call(functools.partial(kernel, (outer, inner, chunks, total)),...  32.4 us
    pallas_call x1, Pallas kernels, in_kernel(): pl.pallas_call(functools.partial(hand_over, pieces), out_shape=(jax.Shape...  0.92 us

profile of v6, /device:TPU:10, one launch (start us, length us, event | category | flops | bytes accessed | tf_op | source)
XLA Modules:
  0.0 33.9 jit_solution(17261628612151031916)
XLA Ops:
  0.6 32.4 %shard_map.59 = (f32[16,128]{1,0:T(8,128)S(1)}, f32[24,32,256]{2,1,0:T(8,128)S(1)}) custom-call(s32[1,24]{1,0:T(1,128)} %bitcast.5, bf16[6144,256]{1,0:T(8,128)(2,1)} %dev_hbm.1, bf16[64,6144]{1,0:T(8,128)(2,1)} %bitcast.3, bf16[4,256,512]{2,1,0:T(8,128)(2,1)} %sens_hbm.1), custom_call_target="tpu_custom_call" | custom-call | flops 1811939328 | bytes 8126464 | tf_op jit(solution)/shard_map/pallas_call | solution.py:290
  33.0 0.9 %shard_map.60 = (f32[16,128]{1,0:T(8,128)}, f32[24,32,256]{2,1,0:T(8,128)}) custom-call(f32[16,128]{1,0:T(8,128)S(1)} %get-tuple-element.6.gram_ref, f32[24,32,256]{2,1,0:T(8,128)S(1)} %get-tuple-element.7.change_ref), custom_call_target="tpu_custom_call" | custom-call | tf_op jit(solution)/shard_map/pallas_call | solution.py:331

commit v7 on v4

--- a/solution.py
+++ b/solution.py
@@ -23,7 +23,7 @@
 
 def kernel(
     dims, ids_hbm, dev_hbm, basis_hbm, sens_hbm, gram_ref, change_ref,
-    ids_ref, dev_v, basis_v, sens_v, turned, blocks, gram_acc, coef_acc, spread_v, keep_v, w_hi, w_lo,
+    ids_ref, dev_v, basis_v, sens_v, turned, blocks, coef_acc, spread_v, keep_v, w_hi, w_lo,
     s1, r1, s2, r2, s3, r3,
     ids_sem, dev_sem, basis_sem, sens_sem, own_sem, a_send, a_recv, c_send, c_recv, x_send, x_recv, z_send, z_recv,
 ):
@@ -50,8 +50,9 @@
 
     far_planes = [(1 - side) * half + (o + e) % half for e in range(half)]
     near_planes = [side * half + (o + e) % half for e in range(half)]
+    planes = [plane for pair in zip(near_planes, far_planes) for plane in pair]
     loads = []
-    for at, plane in enumerate(far_planes + near_planes):
+    for at, plane in enumerate(planes):
         here = pl.ds(pl.multiple_of(plane * span, span), span)
         loads.append(pltpu.make_async_copy(sens_hbm.at[:, :, here], sens_v.at[:, :, here], sens_sem.at[at]))
         loads[-1].start()
@@ -61,7 +62,7 @@
     basis_load.start()
 
     def dev_load(c):
-        at = pl.ds(pl.multiple_of(c * part, part), part)
+        at = pl.ds(c * part, part)
         return pltpu.make_async_copy(dev_hbm.at[at], dev_v.at[at], dev_sem.at[c])
 
     for c in range(chunks):
@@ -85,28 +86,33 @@
             recv_sem=a_recv.at[peer], device_id=(peer, core), device_id_type=MESH,
         )
 
-    crossing = [block_to(plane * inner + (i + e) % inner) for plane in far_planes for e in range(inner)]
-    early = len(crossing) - inner
-    for at, plane in enumerate(far_planes):
+    inside = [plane * inner + (i + e) % inner for plane in near_planes for e in range(inner)][1:]
+    crossing = [plane * inner + (i + e) % inner for plane in far_planes for e in range(inner)]
+    sent = [block_to(peer) for pair in zip(crossing, inside + [None]) for peer in pair if peer is not None]
+    swapped = [sent[at ^ 1] for at in range(len(sent) - 1)] + sent[-1:]
+    done = 0
+
+    def send(amount):
+        nonlocal done
+        here = slice(done, done + amount)
+        done += amount
+        for kind, copies in ((0, sent[here]), (1, swapped[here])):
+            @pl.when(core == kind)
+            def _():
+                for copy in copies:
+                    copy.start()
+
+    for at, plane in enumerate(planes):
         loads[at].wait()
         turn(plane)
-        if at == 0:
+        if at == 1:
             pl.semaphore_wait(barrier, count)
-        for copy in crossing[at * inner:min((at + 1) * inner, early)]:
-            copy.start()
-    sent = []
-    for at, plane in reversed(list(enumerate(near_planes))):
-        loads[half + at].wait()
-        turn(plane)
-        for e in range(inner):
-            if at == 0 and e == 0:
-                continue
-            sent.append(block_to(plane * inner + (i + e) % inner))
-            sent[-1].start()
+            send(4)
     mine = pltpu.make_async_copy(
         turned.at[:, pl.ds(pl.multiple_of(me * cols, cols), cols), :], blocks.at[me], own_sem
     )
     mine.start()
+    send(2)
 
     spread_v[...] = (
         lax.broadcasted_iota(jnp.int32, spread_v.shape, 1) // GROUP == lax.broadcasted_iota(jnp.int32, spread_v.shape, 0)
@@ -116,19 +122,16 @@
         == lax.broadcasted_iota(jnp.int32, keep_v.shape, 1) % GROUP
     ).astype(F32).astype(BF16)
 
-    gram_acc[...] = jnp.zeros_like(gram_acc)
-    coef_acc[...] = jnp.zeros_like(coef_acc)
     basis_load.wait()
-
-    def accumulate(c, carry):
+    gram, coef = 0.0, 0.0
+    for c in range(chunks):
         dev_load(c).wait()
-        start = pl.multiple_of(c * part, part)
-        block = dev_v[pl.ds(start, part), :]
-        gram_acc[...] += jnp.dot(block.T, block, preferred_element_type=F32)
-        coef_acc[0:shapes, :] += jnp.dot(basis_v[:, pl.ds(start, part)], block, preferred_element_type=F32)
-        return carry
-
-    lax.fori_loop(0, chunks, accumulate, 0)
+        at = slice(c * part, (c + 1) * part)
+        block = dev_v[at, :]
+        gram = gram + jnp.dot(block.T, block, preferred_element_type=F32)
+        coef = coef + jnp.dot(basis_v[:, at], block, preferred_element_type=F32)
+    coef_acc[0:shapes, :] = coef
+    coef_acc[shapes:, :] = jnp.zeros_like(coef_acc[shapes:, :])
 
     wide = coef_acc.shape[0]
     ids_load.wait()
@@ -137,7 +140,6 @@
     ids_col = jnp.sum(jnp.where(square, ids, 0.0), axis=1, keepdims=True)
     lane = lax.broadcasted_iota(jnp.int32, (reals, blades), 1).astype(F32)
     chosen = jnp.where(ids_col == lane, 1.0, 0.0).astype(F32)
-    gram = gram_acc[...]
     diagonal = lax.broadcasted_iota(jnp.int32, gram.shape, 0) == lax.broadcasted_iota(jnp.int32, gram.shape, 1)
     squares = jnp.sum(jnp.where(diagonal, gram, 0.0), axis=0, keepdims=True)
     energy = jnp.sum(chosen * squares, axis=1, keepdims=True)
@@ -155,6 +157,7 @@
         device_id=(me, 1 - core), device_id_type=MESH,
     )
     over.start()
+    send(2)
     over.wait_recv()
 
     body = outer * gram_rows
@@ -176,6 +179,7 @@
             )
         )
         plane_sent[-1].start()
+    send(2)
     value = s2[i]
     for e in range(1, inner):
         j = (i + e) % inner
@@ -198,8 +202,7 @@
             )
         )
         out_sent[-1].start()
-    for copy in crossing[early:]:
-        copy.start()
+    send(len(sent) - done)
     value = s3[o]
     for e in range(1, outer):
         q = (o + e) % outer
@@ -222,7 +225,7 @@
 
     mine.wait()
     step = inner * own * GROUP
-    for at, plane in enumerate(near_planes + far_planes):
+    for at, plane in enumerate(planes):
         for e in range(inner):
             if at == 0 and e == 0:
                 continue
@@ -242,7 +245,7 @@
                 change_ref[:, here, :] += term
 
     over.wait_send()
-    for copy in crossing + sent + plane_sent + out_sent:
+    for copy in sent + plane_sent + out_sent:
         copy.wait_send()
 
 
@@ -268,7 +271,7 @@
     outer, inner = split_of(count)
     cols = order // count
     gram_rows, gram_cols = blades // count, blades // cores
-    chunks = 12
+    chunks = 4
     wide = 2 * shapes
     total = float(points * count * cores)
     hbm = pl.BlockSpec(memory_space=pltpu.HBM)
@@ -288,7 +291,6 @@
             pltpu.VMEM((own, rows, order), BF16),
             pltpu.VMEM((own, order, rows), BF16),
             pltpu.VMEM((count, own, cols, rows), BF16),
-            pltpu.VMEM((blades, blades), F32),
             pltpu.VMEM((wide, blades), F32),
             pltpu.VMEM((wide, shapes * GROUP), BF16),
             pltpu.VMEM((reals * GROUP, shapes * GROUP), BF16),
@@ -369,7 +371,7 @@
         and rows % 128 == 0
         and (order // count * inner) % 128 == 0
         and (inner * own * GROUP) % 128 == 0
-        and points % (12 * 128) == 0
+        and points % (4 * 128) == 0
         and blade_ids.shape[0] % 8 == 0
     )
     run = in_kernel if fits else with_collectives

time: 35.2 us -> 32.5 us (0.923)
  the two profiles are of different devices: /device:TPU:11 before, /device:TPU:0 now
where the time goes in v7:
time: 32.5 us; the launch traced here: 32.2 us
  Pallas kernels  31.6 us (97%)
  between operations  0.64 us (2%)
    pallas_call x1, Pallas kernels, in_kernel(): pl.pallas_call(functools.partial(kernel, (outer, inner, chunks, total)),...  30.7 us
    pallas_call x1, Pallas kernels, in_kernel(): pl.pallas_call(functools.partial(hand_over, pieces), out_shape=(jax.Shape...  0.92 us

profile of v7, /device:TPU:0, one launch (start us, length us, event | category | flops | bytes accessed | tf_op | source)
XLA Modules:
  0.0 32.2 jit_solution(15913628382993545758)
XLA Ops:
  0.6 30.7 %shard_map.59 = (f32[16,128]{1,0:T(8,128)S(1)}, f32[24,32,256]{2,1,0:T(8,128)S(1)}) custom-call(s32[1,24]{1,0:T(1,128)} %bitcast.5, bf16[6144,256]{1,0:T(8,128)(2,1)} %dev_hbm.1, bf16[64,6144]{1,0:T(8,128)(2,1)} %bitcast.3, bf16[4,256,512]{2,1,0:T(8,128)(2,1)} %sens_hbm.1), custom_call_target="tpu_custom_call" | custom-call | flops 1811939328 | bytes 8126464 | tf_op jit(solution)/shard_map/pallas_call | solution.py:282
  31.3 0.9 %shard_map.60 = (f32[16,128]{1,0:T(8,128)}, f32[24,32,256]{2,1,0:T(8,128)}) custom-call(f32[16,128]{1,0:T(8,128)S(1)} %get-tuple-element.6.gram_ref, f32[24,32,256]{2,1,0:T(8,128)S(1)} %get-tuple-element.7.change_ref), custom_call_target="tpu_custom_call" | custom-call | tf_op jit(solution)/shard_map/pallas_call | solution.py:322

commit v8 on v7

--- a/solution.py
+++ b/solution.py
@@ -43,19 +43,24 @@
     gram_rows, gram_cols = gram_ref.shape
     span = cols * inner
 
+    far_planes = [(1 - side) * half + (o + e) % half for e in range(half)]
+    near_planes = [side * half + (o + e) % half for e in range(half)]
+    planes = [plane for pair in zip(near_planes, far_planes) for plane in pair]
+    turns = [
+        plane for n, f in zip(near_planes, far_planes) for plane in (core * n + (1 - core) * f, core * f + (1 - core) * n)
+    ]
+    loads = []
+    for at, plane in enumerate(turns):
+        here = pl.ds(pl.multiple_of(plane * span, span), span)
+        loads.append(pltpu.make_async_copy(sens_hbm.at[:, :, here], sens_v.at[:, :, here], sens_sem.at[at]))
+    loads[0].start()
+
     barrier = pltpu.get_barrier_semaphore()
     for d in range(1, count):
         pl.semaphore_signal(barrier, inc=1, device_id=((me + d) % count, core), device_id_type=MESH)
     pl.semaphore_signal(barrier, inc=1, device_id=(me, 1 - core), device_id_type=MESH)
-
-    far_planes = [(1 - side) * half + (o + e) % half for e in range(half)]
-    near_planes = [side * half + (o + e) % half for e in range(half)]
-    planes = [plane for pair in zip(near_planes, far_planes) for plane in pair]
-    loads = []
-    for at, plane in enumerate(planes):
-        here = pl.ds(pl.multiple_of(plane * span, span), span)
-        loads.append(pltpu.make_async_copy(sens_hbm.at[:, :, here], sens_v.at[:, :, here], sens_sem.at[at]))
-        loads[-1].start()
+    for load in loads[1:]:
+        load.start()
     ids_load = pltpu.make_async_copy(ids_hbm, ids_ref, ids_sem)
     ids_load.start()
     basis_load = pltpu.make_async_copy(basis_hbm, basis_v, basis_sem)
@@ -86,10 +91,15 @@
             recv_sem=a_recv.at[peer], device_id=(peer, core), device_id_type=MESH,
         )
 
-    inside = [plane * inner + (i + e) % inner for plane in near_planes for e in range(inner)][1:]
-    crossing = [plane * inner + (i + e) % inner for plane in far_planes for e in range(inner)]
+    pairs = inner // 2
+    peers = [(i // 2 + h) % pairs * 2 + (i + b) % 2 for h in range(pairs) for b in range(2)]
+
+    inside = [plane * inner + peer for plane in near_planes for peer in peers][1:]
+    crossing = [plane * inner + peer for plane in far_planes for peer in peers]
     sent = [block_to(peer) for pair in zip(crossing, inside + [None]) for peer in pair if peer is not None]
     swapped = [sent[at ^ 1] for at in range(len(sent) - 1)] + sent[-1:]
+    sent[1], sent[2] = sent[2], sent[1]
+    swapped[1], swapped[2] = swapped[2], swapped[1]
     done = 0
 
     def send(amount):
@@ -102,12 +112,13 @@
                 for copy in copies:
                     copy.start()
 
-    for at, plane in enumerate(planes):
+    for at, plane in enumerate(turns):
         loads[at].wait()
         turn(plane)
-        if at == 1:
+        if at == 0:
             pl.semaphore_wait(barrier, count)
-            send(4)
+        if at < 2:
+            send(2)
     mine = pltpu.make_async_copy(
         turned.at[:, pl.ds(pl.multiple_of(me * cols, cols), cols), :], blocks.at[me], own_sem
     )
@@ -224,25 +235,25 @@
     w_lo[...] = jnp.dot(lo, spread, preferred_element_type=F32).astype(BF16) * keep_v[...]
 
     mine.wait()
-    step = inner * own * GROUP
+    step = 2 * own * GROUP
     for at, plane in enumerate(planes):
-        for e in range(inner):
-            if at == 0 and e == 0:
-                continue
-            block_from(plane * inner + (i + e) % inner).wait_recv()
-        lanes = pl.ds(pl.multiple_of(plane * step, step), step)
-        left_hi, left_lo = w_hi[:, lanes], w_lo[:, lanes]
-        for g in range(cols // GROUP):
-            here = slice(g * GROUP, (g + 1) * GROUP)
-            right = blocks[pl.ds(plane * inner, inner), :, here, :].reshape(step, rows)
-            term = jnp.dot(left_hi, right, preferred_element_type=F32) + jnp.dot(
-                left_lo, right, preferred_element_type=F32
-            )
-            term = term.reshape(reals, GROUP, rows)
-            if at == 0:
-                change_ref[:, here, :] = term
-            else:
-                change_ref[:, here, :] += term
+        for h in range(pairs):
+            pair = plane * pairs + (i // 2 + pairs - h) % pairs
+            for b in range(2):
+                if at == 0 and h == 0 and b == 0:
+                    continue
+                block_from(pair * 2 + (i + b) % 2).wait_recv()
+            lanes = pl.ds(pl.multiple_of(pair * step, step), step)
+            left = jnp.concatenate([w_hi[:, lanes], w_lo[:, lanes]], axis=1)
+            for g in range(cols // GROUP):
+                here = slice(g * GROUP, (g + 1) * GROUP)
+                right = blocks[pl.ds(pair * 2, 2), :, here, :].reshape(step, rows)
+                right = jnp.concatenate([right, right], axis=0)
+                term = jnp.dot(left, right, preferred_element_type=F32).reshape(reals, GROUP, rows)
+                if at == 0 and h == 0:
+                    change_ref[:, here, :] = term
+                else:
+                    change_ref[:, here, :] += term
 
     over.wait_send()
     for copy in sent + plane_sent + out_sent:
@@ -370,7 +381,8 @@
         and (blades // cores) % 128 == 0
         and rows % 128 == 0
         and (order // count * inner) % 128 == 0
-        and (inner * own * GROUP) % 128 == 0
+        and inner % 2 == 0
+        and (2 * own * GROUP) % 128 == 0
         and points % (4 * 128) == 0
         and blade_ids.shape[0] % 8 == 0
     )

time: 32.5 us -> 32.9 us (1.012)
  no operation moved by 1% of the time
where the time goes in v8:
time: 32.9 us; the launch traced here: 32.3 us
  Pallas kernels  31.7 us (96%)
  between operations  0.64 us (2%)
    pallas_call x1, Pallas kernels, in_kernel(): pl.pallas_call(functools.partial(kernel, (outer, inner, chunks, total)),...  30.8 us
    pallas_call x1, Pallas kernels, in_kernel(): pl.pallas_call(functools.partial(hand_over, pieces), out_shape=(jax.Shape...  0.92 us

profile of v8, /device:TPU:0, one launch (start us, length us, event | category | flops | bytes accessed | tf_op | source)
XLA Modules:
  0.0 32.3 jit_solution(2983401011835990273)
XLA Ops:
  0.6 30.8 %shard_map.59 = (f32[16,128]{1,0:T(8,128)S(1)}, f32[24,32,256]{2,1,0:T(8,128)S(1)}) custom-call(s32[1,24]{1,0:T(1,128)} %bitcast.5, bf16[6144,256]{1,0:T(8,128)(2,1)} %dev_hbm.1, bf16[64,6144]{1,0:T(8,128)(2,1)} %bitcast.3, bf16[4,256,512]{2,1,0:T(8,128)(2,1)} %sens_hbm.1), custom_call_target="tpu_custom_call" | custom-call | flops 1811939328 | bytes 8126464 | tf_op jit(solution)/shard_map/pallas_call | solution.py:293
  31.4 0.9 %shard_map.60 = (f32[16,128]{1,0:T(8,128)}, f32[24,32,256]{2,1,0:T(8,128)}) custom-call(f32[16,128]{1,0:T(8,128)S(1)} %get-tuple-element.6.gram_ref, f32[24,32,256]{2,1,0:T(8,128)S(1)} %get-tuple-element.7.change_ref), custom_call_target="tpu_custom_call" | custom-call | tf_op jit(solution)/shard_map/pallas_call | solution.py:333

commit v9 on v8

--- a/solution.py
+++ b/solution.py
@@ -24,8 +24,9 @@
 def kernel(
     dims, ids_hbm, dev_hbm, basis_hbm, sens_hbm, gram_ref, change_ref,
     ids_ref, dev_v, basis_v, sens_v, turned, blocks, coef_acc, spread_v, keep_v, w_hi, w_lo,
-    s1, r1, s2, r2, s3, r3,
+    s1, r1, s2, r2, s3, r3, s4, r4,
     ids_sem, dev_sem, basis_sem, sens_sem, own_sem, a_send, a_recv, c_send, c_recv, x_send, x_recv, z_send, z_recv,
+    m_send, m_recv,
 ):
     outer, inner, chunks, total = dims
     count = outer * inner
@@ -200,31 +201,48 @@
         ).wait_recv()
         value = value + r2[j]
 
-    for q in range(outer):
-        s3[q, 0:gram_rows, :] = value[q * gram_rows:(q + 1) * gram_rows, :]
-        s3[q, gram_rows:gram_rows + reals, :] = value[body:body + reals, :]
+    r2[i] = value
+    place_in_half = o % half
+    for n in range(half):
+        for at, plane in enumerate((side * half + n, (1 - side) * half + n)):
+            there = pl.ds(pl.multiple_of(plane * gram_rows, gram_rows), gram_rows)
+            s3[n, at * gram_rows:(at + 1) * gram_rows, :] = r2[i, there, :]
+        s3[n, 2 * gram_rows:2 * gram_rows + reals, :] = value[body:body + reals, :]
     out_sent = []
-    for e in range(1, outer):
-        q = (o + e) % outer
+    for e in range(1, half):
+        n = (place_in_half + e) % half
         out_sent.append(
             pltpu.make_async_remote_copy(
-                src_ref=s3.at[q], dst_ref=r3.at[o], send_sem=z_send.at[q], recv_sem=z_recv.at[o],
-                device_id=(q * inner + i, core), device_id_type=MESH,
+                src_ref=s3.at[n], dst_ref=r3.at[place_in_half], send_sem=z_send.at[n],
+                recv_sem=z_recv.at[place_in_half],
+                device_id=((side * half + n) * inner + i, core), device_id_type=MESH,
             )
         )
         out_sent[-1].start()
+    send(1)
+    value = s3[place_in_half]
+    for e in range(1, half):
+        n = (place_in_half + e) % half
+        pltpu.make_async_remote_copy(
+            src_ref=s3.at[n], dst_ref=r3.at[n], send_sem=z_send.at[n], recv_sem=z_recv.at[n],
+            device_id=((side * half + n) * inner + i, core), device_id_type=MESH,
+        ).wait_recv()
+        value = value + r3[n]
+
+    s4[0:gram_rows, :] = value[gram_rows:2 * gram_rows, :]
+    s4[gram_rows:gram_rows + reals, :] = value[2 * gram_rows:2 * gram_rows + reals, :]
+    out_sent.append(
+        pltpu.make_async_remote_copy(
+            src_ref=s4, dst_ref=r4, send_sem=m_send, recv_sem=m_recv,
+            device_id=((o + half) % outer * inner + i, core), device_id_type=MESH,
+        )
+    )
+    out_sent[-1].start()
     send(len(sent) - done)
-    value = s3[o]
-    for e in range(1, outer):
-        q = (o + e) % outer
-        pltpu.make_async_remote_copy(
-            src_ref=s3.at[q], dst_ref=r3.at[q], send_sem=z_send.at[q], recv_sem=z_recv.at[q],
-            device_id=(q * inner + i, core), device_id_type=MESH,
-        ).wait_recv()
-        value = value + r3[q]
-    gram_ref[...] = value[0:gram_rows, :] / total
-
-    packed = value[gram_rows:gram_rows + reals, :]
+    out_sent[-1].wait_recv()
+    gram_ref[...] = (value[0:gram_rows, :] + r4[0:gram_rows, :]) / total
+    packed = value[2 * gram_rows:2 * gram_rows + reals, :] + r4[gram_rows:gram_rows + reals, :]
+
     moved = pltpu.roll(packed, wide - shapes, 1)
     weights = jnp.where(place < shapes, packed / jnp.sqrt(jnp.where(place < shapes, moved, 0.0) / total + EPS), 0.0)
     tall = jnp.broadcast_to(weights[:, None, :], (reals, GROUP, wide)).reshape(reals * GROUP, wide)
@@ -311,11 +329,13 @@
             pltpu.VMEM((blades + reals, gram_cols), F32),
             pltpu.VMEM((inner, body + reals, gram_cols), F32),
             pltpu.VMEM((inner, body + reals, gram_cols), F32),
-            pltpu.VMEM((outer, gram_rows + reals, gram_cols), F32),
-            pltpu.VMEM((outer, gram_rows + reals, gram_cols), F32),
+            pltpu.VMEM((outer // 2, 2 * gram_rows + reals, gram_cols), F32),
+            pltpu.VMEM((outer // 2, 2 * gram_rows + reals, gram_cols), F32),
+            pltpu.VMEM((gram_rows + reals, gram_cols), F32),
+            pltpu.VMEM((gram_rows + reals, gram_cols), F32),
             sem, sem((chunks,)), sem, sem((outer,)), sem,
             sem((count,)), sem((count,)), sem, sem,
-            sem((inner,)), sem((inner,)), sem((outer,)), sem((outer,)),
+            sem((inner,)), sem((inner,)), sem((outer // 2,)), sem((outer // 2,)), sem, sem,
         ],
         compiler_params=pltpu.CompilerParams(
             collective_id=0, has_side_effects=True, vmem_limit_bytes=32 * 1024 * 1024

time: 32.9 us -> 32.8 us (level); the launches traced: 32.3 us -> 32.6 us
  no operation moved by 1% of the time
where the time goes in v9:
time: 32.8 us; the launch traced here: 32.6 us
  Pallas kernels  32 us (98%)
  between operations  0.64 us (2%)
    pallas_call x1, Pallas kernels, in_kernel(): pl.pallas_call(functools.partial(kernel, (outer, inner, chunks, total)),...  31.1 us
    pallas_call x1, Pallas kernels, in_kernel(): pl.pallas_call(functools.partial(hand_over, pieces), out_shape=(jax.Shape...  0.92 us

profile of v9, /device:TPU:0, one launch (start us, length us, event | category | flops | bytes accessed | tf_op | source)
XLA Modules:
  0.0 32.6 jit_solution(10311680890020788133)
XLA Ops:
  0.6 31.1 %shard_map.59 = (f32[16,128]{1,0:T(8,128)S(1)}, f32[24,32,256]{2,1,0:T(8,128)S(1)}) custom-call(s32[1,24]{1,0:T(1,128)} %bitcast.5, bf16[6144,256]{1,0:T(8,128)(2,1)} %dev_hbm.1, bf16[64,6144]{1,0:T(8,128)(2,1)} %bitcast.3, bf16[4,256,512]{2,1,0:T(8,128)(2,1)} %sens_hbm.1), custom_call_target="tpu_custom_call" | custom-call | flops 1811939328 | bytes 8126464 | tf_op jit(solution)/shard_map/pallas_call | solution.py:311
  31.7 0.9 %shard_map.60 = (f32[16,128]{1,0:T(8,128)}, f32[24,32,256]{2,1,0:T(8,128)}) custom-call(f32[16,128]{1,0:T(8,128)S(1)} %get-tuple-element.6.gram_ref, f32[24,32,256]{2,1,0:T(8,128)S(1)} %get-tuple-element.7.change_ref), custom_call_target="tpu_custom_call" | custom-call | tf_op jit(solution)/shard_map/pallas_call | solution.py:353
